TPU v7x, 32 devices: a whole 2x2x4 slice. The times are simulated.
32 devices in a mesh: depth: 2 (over core), tile: 16 (over z, y, x).
Axes of the slice: x: 2, y: 2, z: 4, core: 2. Of those that a mesh axis runs over, the one named last changes fastest.
Arguments:
- transmission: bfloat16 [2, 2, 2048, 4096], P('depth', None, None, 'tile')
- chirp_taps: float32 [5], replicated, may hold values from -0.06 to 0.06
- probe_field: float32 [2, 256, 256], replicated, may hold values from -6 to 6
- records: bfloat16 [16, 2, 256, 256], P('tile'), may hold values from 0 to 2
- pos_row: int32 [16, 2], P('tile'), may hold values from 0 to 1792
- pos_col: int32 [16, 2], P('tile'), may hold values from 0 to 255
- counts: int32 [16], P('tile'), may hold values from 1 to 2, as said below
Outputs:
- gradient: bfloat16 [2, 2, 2048, 4096], P('depth', None, None, 'tile')
Inputs may be any that keep to these rules, and one draw needn't show every extreme that they name: Slots 0 to counts[t] - 1 of tile t are live; some tile has 2.
All inputs are finite; a program needn't handle non-finite values.
Results may differ from a plain program's by a relative error of at most 0.011.
Values may be sent and summed in bfloat16 or wider, within the bound.
A program may use at most 64 MiB of HBM per device.

v0:
```python
import math

import jax
import jax.numpy as jnp
from jax import lax
from jax.sharding import PartitionSpec as P


def from_behind(block, axis, distance):
    devices = range(lax.axis_size(axis))
    route = [((i - distance) % len(devices), i) for i in devices]
    return lax.ppermute(block, axis, route)


def passed_along(shard, axis, by):
    devices = lax.axis_size(axis)
    pairs = [(i, i + by) for i in range(devices) if 0 <= i + by < devices]
    return lax.ppermute(shard, axis, pairs)


def spread_taps(values, chirp_taps, axis_pos):
    reach = chirp_taps.shape[0] - 1
    length = values.shape[axis_pos]
    widths = [(0, 0)] * values.ndim
    widths[axis_pos] = (reach, reach)
    padded = jnp.pad(values, widths)
    total = chirp_taps[0] * values
    for offset in range(1, reach + 1):
        upper = lax.slice_in_dim(padded, reach + offset, reach + offset + length, axis=axis_pos)
        lower = lax.slice_in_dim(padded, reach - offset, reach - offset + length, axis=axis_pos)
        total = total + chirp_taps[offset] * (upper + lower)
    return total


def propagate(wavefield, chirp_taps, sign_value):
    for axis_neg in (-1, -2):
        real_part = wavefield[..., 0, :, :]
        imag_part = wavefield[..., 1, :, :]
        axis_pos = real_part.ndim + axis_neg
        new_real = real_part - sign_value * spread_taps(imag_part, chirp_taps, axis_pos)
        new_imag = imag_part + sign_value * spread_taps(real_part, chirp_taps, axis_pos)
        wavefield = jnp.stack([new_real, new_imag], axis=-3)
    return wavefield


def complex_mul(first, second):
    ar, ai = (first[..., 0, :, :], first[..., 1, :, :])
    br, bi = (second[..., 0, :, :], second[..., 1, :, :])
    return jnp.stack([ar * br - ai * bi, ar * bi + ai * br], axis=-3)


def conj_mul(first, second):
    ar, ai = (first[..., 0, :, :], first[..., 1, :, :])
    br, bi = (second[..., 0, :, :], second[..., 1, :, :])
    return jnp.stack([ar * br + ai * bi, ar * bi - ai * br], axis=-3)


def group_forward(wavefield, windows, chirp_taps):
    incoming = [wavefield]
    wavefield = propagate(complex_mul(windows[:, 0], wavefield), chirp_taps, 1.0)
    return (wavefield, jnp.stack(incoming, axis=1))


def group_adjoint(adjoint, windows, incoming, chirp_taps):
    terms = [None] * windows.shape[1]
    for number in reversed(range(windows.shape[1])):
        pulled = propagate(adjoint, chirp_taps, -1.0)
        terms[number] = conj_mul(incoming[:, number], pulled)
        adjoint = conj_mul(windows[:, number], pulled)
    return (adjoint, jnp.stack(terms, axis=1))


def dft_tables(length):
    indices = jnp.arange(length, dtype=jnp.int32)
    product = indices[:, None] * indices[None, :] % length
    angle = product.astype(jnp.float32) * (2.0 * math.pi / length)
    factor = 1.0 / math.sqrt(length)
    return (
        (jnp.cos(angle) * factor).astype(jnp.bfloat16),
        (jnp.sin(angle) * factor).astype(jnp.bfloat16),
    )


def left_mul(matrix, values):
    return jnp.einsum("jk,bkl->bjl", matrix, values, preferred_element_type=jnp.float32)


def right_mul(values, matrix):
    return jnp.einsum("bjk,kl->bjl", values, matrix, preferred_element_type=jnp.float32)


def far_field(exit_wave, intensity, live_mask):
    cos_table, sin_table = dft_tables(exit_wave.shape[-1])
    exit_real = exit_wave[:, 0].astype(jnp.bfloat16)
    exit_imag = exit_wave[:, 1].astype(jnp.bfloat16)
    half_real = (left_mul(cos_table, exit_real) + left_mul(sin_table, exit_imag)).astype(
        jnp.bfloat16
    )
    half_imag = (left_mul(cos_table, exit_imag) - left_mul(sin_table, exit_real)).astype(
        jnp.bfloat16
    )
    far_real = right_mul(half_real, cos_table) + right_mul(half_imag, sin_table)
    far_imag = right_mul(half_imag, cos_table) - right_mul(half_real, sin_table)
    misfit = (
        far_real * far_real + far_imag * far_imag - intensity.astype(jnp.float32)
    ) * live_mask[:, None, None]
    grad_real = (misfit * far_real).astype(jnp.bfloat16)
    grad_imag = (misfit * far_imag).astype(jnp.bfloat16)
    back_real = (left_mul(cos_table, grad_real) - left_mul(sin_table, grad_imag)).astype(
        jnp.bfloat16
    )
    back_imag = (left_mul(cos_table, grad_imag) + left_mul(sin_table, grad_real)).astype(
        jnp.bfloat16
    )
    adj_real = right_mul(back_real, cos_table) - right_mul(back_imag, sin_table)
    adj_imag = right_mul(back_imag, cos_table) + right_mul(back_real, sin_table)
    return jnp.stack([adj_real, adj_imag], axis=1)


def on_device(transmission, chirp_taps, probe_field, records, pos_row, pos_col, counts):
    slices_here = transmission.shape[0]
    tile_cols = transmission.shape[3]
    side = probe_field.shape[-1]
    slots = pos_row.shape[1]
    zero_index = jnp.int32(0)
    neighbor = from_behind(transmission, "tile", -1)
    extended = jnp.concatenate([transmission, neighbor], axis=3)

    def window_at(row_start, col_start):
        return lax.dynamic_slice(
            extended, (zero_index, zero_index, row_start, col_start), (slices_here, 2, side, side)
        )

    windows = jax.vmap(window_at)(pos_row[0], pos_col[0]).astype(jnp.float32)
    live_mask = (jnp.arange(slots, dtype=jnp.int32) < counts[0]).astype(jnp.float32)
    depth_count = lax.axis_size("depth")
    my_depth = lax.axis_index("depth")
    num_blocks = slots // slots
    total_steps = depth_count + num_blocks - 1
    probe_batch = jnp.broadcast_to(probe_field, (slots, 2, side, side))
    empty_wire = jnp.zeros((slots, 2, side, side), jnp.bfloat16)
    stored_start = jnp.zeros((slots, slices_here, 2, side, side), jnp.float32)

    def remember(stored, incoming, start_row):
        return lax.dynamic_update_slice_in_dim(stored, incoming, start_row, 0)

    def advance(counter, carried):
        received, inputs, stored, exits = carried
        block_id = counter - my_depth
        active = (block_id >= 0) & (block_id < num_blocks)
        start_row = jnp.clip(block_id, 0, num_blocks - 1) * slots
        entry = jnp.where(my_depth == 0, probe_batch, received.astype(jnp.float32))

        def advance_run_group(operand):
            leaving, incoming = group_forward(entry, windows, chirp_taps)
            new_stored = remember(stored, incoming, start_row)
            return (leaving.astype(jnp.bfloat16), entry, new_stored, leaving)

        def advance_skip_group(operand):
            return (empty_wire, inputs, stored, exits)

        return lax.cond(active, advance_run_group, advance_skip_group, 0)

    def forward_step(counter, carried):
        outgoing, inputs, stored, exits = advance(counter, carried)
        received = passed_along(outgoing, "depth", 1)
        return (received, inputs, stored, exits)

    wave_zeros = jnp.zeros((slots, 2, side, side), jnp.float32)
    carried = lax.fori_loop(
        0, total_steps - 1, forward_step, (empty_wire, wave_zeros, stored_start, wave_zeros)
    )
    unused, inputs, stored, exits = advance(total_steps - 1, carried)

    def bottom_work(operand):
        return far_field(exits, records[0], live_mask)

    def bottom_skip(operand):
        return wave_zeros

    bottom = lax.cond(my_depth == depth_count - 1, bottom_work, bottom_skip, 0)

    def retreat(counter, carried):
        received, grads = carried
        block_id = counter - (depth_count - 1 - my_depth)
        active = (block_id >= 0) & (block_id < num_blocks)
        start_row = jnp.clip(block_id, 0, num_blocks - 1) * slots
        entry = jnp.where(my_depth == depth_count - 1, bottom, received.astype(jnp.float32))

        def retreat_run_group(operand):
            leaving, terms = group_adjoint(entry, windows, stored, chirp_taps)
            return (
                leaving.astype(jnp.bfloat16),
                lax.dynamic_update_slice_in_dim(grads, terms, start_row, 0),
            )

        def retreat_skip_group(operand):
            return (empty_wire, grads)

        return lax.cond(active, retreat_run_group, retreat_skip_group, 0)

    def backward_step(counter, carried):
        outgoing, grads = retreat(counter, carried)
        received = passed_along(outgoing, "depth", -1)
        return (received, grads)

    grads_start = jnp.zeros((slots, slices_here, 2, side, side), jnp.float32)
    carried = lax.fori_loop(0, total_steps - 1, backward_step, (empty_wire, grads_start))
    unused, grads = retreat(total_steps - 1, carried)
    accum = jnp.zeros((slices_here, 2, transmission.shape[2], 2 * tile_cols), jnp.float32)
    for slot in range(slots):
        corner = (zero_index, zero_index, pos_row[0, slot], pos_col[0, slot])
        current = lax.dynamic_slice(accum, corner, (slices_here, 2, side, side))
        accum = lax.dynamic_update_slice(accum, current + grads[slot], corner)
    from_left = from_behind(accum[..., tile_cols:].astype(jnp.bfloat16), "tile", 1).astype(
        jnp.float32
    )
    return (accum[..., :tile_cols] + from_left).astype(jnp.bfloat16)


def solution(mesh):
    in_specs = (
        P("depth", None, None, "tile"),
        P(),
        P(),
        P("tile", None, None, None),
        P("tile", None),
        P("tile", None),
        P("tile"),
    )
    out_specs = P("depth", None, None, "tile")
    return jax.shard_map(
        on_device, mesh=mesh, in_specs=in_specs, out_specs=out_specs, check_vma=False
    )
```

profile of v0, /device:TPU:0, one launch (start us, length us, event | category | flops | bytes accessed | tf_op | source)
XLA Modules:
  0.0 227.1 jit_solution(1898526685386873121)
XLA Ops:
  0.0 6.9 %collective-permute-start = (bf16[1,2,2048,256]{3,2,1,0:T(8,128)(2,1)}, bf16[1,2,2048,256]{3,2,1,0:T(8,128)(2,1)}, u32[]{:S(2)}, u32[]{:S(2)}) collective-permute-start(bf16[1,2,2048,256]{3,2,1,0:T(8,128)(2,1)} %param.17), channel_id=1, source_target_pairs={{1,0},{2,1},{3,2},{4,3},{5,4},{6,5},{7,6},{8,7},{9,8},{10,9},{11,1... | collective-permute-start | bytes 6291464 | tf_op jit(solution)/shard_map/ppermute | solution.py:12
  8.7 43.4 %collective-permute-done = bf16[1,2,2048,256]{3,2,1,0:T(8,128)(2,1)} collective-permute-done((bf16[1,2,2048,256]{3,2,1,0:T(8,128)(2,1)}, bf16[1,2,2048,256]{3,2,1,0:T(8,128)(2,1)}, u32[]{:S(2)}, u32[]{:S(2)}) %collective-permute-start) | collective-permute-done | bytes 2097184 | tf_op jit(solution)/shard_map/ppermute | solution.py:12
  52.1 4.5 %pad_maximum_fusion.5 = bf16[1,2,2048,512]{3,2,1,0:T(8,128)(2,1)} fusion(bf16[1,2,2048,256]{3,2,1,0:T(8,128)(2,1)} %collective-permute-done, bf16[1,2,2048,256]{3,2,1,0:T(8,128)(2,1)} %param.17), kind=kLoop, calls=%fused_computation.361 | loop fusion | flops 8388608 | bytes 8388608 | tf_op jit(solution)/shard_map/concatenate | solution.py:127
  56.6 6.2 %while.4 = (s32[]{:T(128)}, bf16[1,2,2048,512]{3,2,1,0:T(8,128)(2,1)}, s32[2,4]{1,0:T(2,128)S(1)}, bf16[2,1,2,256,256]{4,3,2,1,0:T(8,128)(2,1)S(1)}, s32[]{:T(128)}) while((s32[]{:T(128)}, bf16[1,2,2048,512]{3,2,1,0:T(8,128)(2,1)}, s32[2,4]{1,0:T(2,128)S(1)}, bf16[2,1,2,256,256]{4,3,2,1,0:T(8,128)(2,1)S(1)}, s32[]{:T(128)}) %tuple.131), condition=%wide.while_cond, body=%wide.while_body.sunk | while | flops 2 | bytes 524421 | solution.py:130
  57.3 2.4 %bitcast_dynamic-update-slice_fusion.2 = bf16[2,1,2,256,256]{4,3,2,1,0:T(8,128)(2,1)S(1)} fusion(bf16[2,1,2,256,256]{4,3,2,1,0:T(8,128)(2,1)S(1)} %get-tuple-element.381, s32[]{:T(128)S(6)} %copy.79, bf16[1,2,2048,512]{3,2,1,0:T(8,128)(2,1)} %get-tuple-element.384, s32[]{:T(128)} %bitcast.256, s32[]{:T(128)} %bitcast.257), kind=kLoop, calls=%fused_computation.356.clone.1 | loop fusion | bytes 524300 | tf_op jit(solution)/shard_map/vmap()/gather
  60.4 2.4 %bitcast_dynamic-update-slice_fusion.2 = bf16[2,1,2,256,256]{4,3,2,1,0:T(8,128)(2,1)S(1)} fusion(bf16[2,1,2,256,256]{4,3,2,1,0:T(8,128)(2,1)S(1)} %get-tuple-element.381, s32[]{:T(128)S(6)} %copy.79, bf16[1,2,2048,512]{3,2,1,0:T(8,128)(2,1)} %get-tuple-element.384, s32[]{:T(128)} %bitcast.256, s32[]{:T(128)} %bitcast.257), kind=kLoop, calls=%fused_computation.356.clone.1 | loop fusion | bytes 524300 | tf_op jit(solution)/shard_map/vmap()/gather
  63.7 1.1 convert_element_type.186
  64.8 15.9 %conditional.5 = (bf16[2,2,256,256]{3,2,0,1:T(8,128)(2,1)S(1)}, f32[2,1,2,256,256]{4,3,2,1,0:T(8,128)}, f32[2,2,256,256]{3,2,0,1:T(8,128)}) conditional(s32[]{:T(128)} %convert_element_type.189, (f32[2,1,2,256,256]{4,3,0,2,1:T(8,128)S(1)}, f32[2,2,256,256]{3,2,0,1:T(8,128)S(1)}) %tuple.62, (f32[2,1,2,256,256]{4,3,2,1,0:T(8,128)S(1)}, pred[]{:T(512)}, ...), branch_computations={%region_0.1_spmd, %region_1.2_spmd} | conditional | flops 9175040 | bytes 18874492 | solution.py:162
  65.6 1.1 broadcast_select_fusion
  66.8 1.1 stack.72
  67.9 4.1 %fusion.19 = (f32[2,256,256]{2,1,0:T(8,128)S(1)}, f32[2,256,256]{2,1,0:T(8,128)S(1)}) fusion(f32[2,256,256]{2,1,0:T(8,128)S(1)} %multiply_subtract_fusion, f32[]{:T(128)} %bitcast.9, f32[]{:T(128)} %bitcast.8, f32[]{:T(128)} %bitcast.7, f32[]{:T(128)} %bitcast.6, f32[]{:T(128)} %bitcast.5, f32[256,256]{1,0:T(8,128)S(1)} %get-tuple-element.303, ...), kind=kLoop, calls=%fused_computation.37 | loop fusion | flops 2228224 | bytes 3145748 | tf_op jit(solution)/shard_map/while/body/eval_jaxpr/cond/branch_1_fun/add | solution.py:41
  72.0 4.1 %subtract_bitcast_fusion = (f32[2,1,256,256]{3,2,0,1:T(8,128)S(1)}, f32[2,256,256]{2,1,0:T(8,128)S(1)}) fusion(f32[2,256,256]{2,1,0:T(8,128)S(1)} %get-tuple-element.285, f32[]{:T(128)} %bitcast.9, f32[]{:T(128)} %bitcast.8, f32[]{:T(128)} %bitcast.7, f32[]{:T(128)} %bitcast.6, f32[]{:T(128)} %bitcast.5, f32[2,256,256]{2,1,0:T(8,128)S(1)} %get-tuple-element.286, ...), kind=kLoop, calls=%fused_computation.47 | loop fusion | flops 4063232 | bytes 3670036 | tf_op jit(solution)/shard_map/while/body/eval_jaxpr/cond/branch_1_fun/stack | solution.py:42
  76.1 3.5 %add_bitcast_fusion = f32[2,1,256,256]{3,2,0,1:T(8,128)S(1)} fusion(f32[2,256,256]{2,1,0:T(8,128)S(1)} %get-tuple-element.285, f32[2,256,256]{2,1,0:T(8,128)S(1)} %get-tuple-element.284, f32[]{:T(128)} %bitcast.9, f32[]{:T(128)} %bitcast.8, f32[]{:T(128)} %bitcast.7, f32[]{:T(128)} %bitcast.6, f32[]{:T(128)} %bitcast.5), kind=kLoop, calls=%fused_computation.46 | loop fusion | flops 1835008 | bytes 1572884 | tf_op jit(solution)/shard_map/while/body/eval_jaxpr/cond/branch_1_fun/stack | solution.py:42
  79.6 1.2 fusion.238
  81.6 2.1 collective-permute-start.1
  84.7 1.1 convert_element_type.190
  86.8 1.1 conditional.7
  86.8 1.1 broadcast_in_dim.31
  88.7 1.3 collective-permute-start.2
  98.8 42.5 %collective-permute-done.2 = bf16[2,2,256,256]{3,2,0,1:T(8,128)(2,1)S(1)} collective-permute-done((bf16[2,2,256,256]{3,2,0,1:T(8,128)(2,1)}, bf16[2,2,256,256]{3,2,0,1:T(8,128)(2,1)S(1)}, u32[]{:S(2)}, u32[]{:S(2)}) %collective-permute-start.2) | collective-permute-done | bytes 524320 | tf_op jit(solution)/shard_map/while/body/eval_jaxpr/ppermute | solution.py:18
  141.4 13.0 %conditional.9 = (f32[1,2,256,256]{3,2,0,1:T(8,128)}, f32[1,2,256,256]{3,2,0,1:T(8,128)}) conditional(s32[]{:T(128)} %convert_element_type.184, f32[2,1,2,256,256]{4,3,0,2,1:T(8,128)S(1)} %get-tuple-element.219, (f32[2,1,2,256,256]{4,3,2,0,1:T(8,128)}, pred[]{:T(512)}, f32[2,2,256,256]{3,2,0,1:T(8,128)}, f32[2,2,256,256]{3,2,0,1:T(8,128)S(1)}, ...), branch_computations={%region_8.9_spmd, %region_9.10_spmd} | conditional | flops 9175040 | bytes 18874464 | solution.py:200
  142.2 1.3 copy_bitcast_fusion.4
  143.6 5.4 %fusion.230 = (f32[2,256,256]{2,1,0:T(8,128)S(1)}, f32[2,256,256]{2,1,0:T(8,128)S(1)}) fusion(f32[2,256,256]{2,1,0:T(8,128)S(1)} %get-tuple-element.333, f32[]{:T(128)} %bitcast.67, f32[]{:T(128)} %bitcast.66, f32[]{:T(128)} %bitcast.65, f32[]{:T(128)} %bitcast.64, f32[]{:T(128)} %bitcast.62, f32[2,2,256,256]{3,2,0,1:T(8,128)S(1)} %broadcast_select_fusion.3, ...), kind=kLoop, calls=%fused_computation.339 | loop fusion | flops 3932160 | bytes 3145748 | tf_op jit(solution)/shard_map/cond/branch_1_fun/add | solution.py:41
  149.0 4.2 %subtract_bitcast_fusion.3 = (f32[2,1,256,256]{3,2,0,1:T(8,128)S(1)}, f32[2,256,256]{2,1,0:T(8,128)S(1)}, f32[2,256,256]{2,1,0:T(8,128)S(1)}) fusion(f32[2,2,256,256]{3,2,0,1:T(8,128)S(1)} %copy_bitcast_fusion.4, f32[2,256,256]{2,1,0:T(8,128)S(1)} %get-tuple-element.332, f32[]{:T(128)} %bitcast.67, f32[]{:T(128)} %bitcast.66, f32[]{:T(128)} %bitcast.65, ...), kind=kLoop, calls=%fused_computation.351 | loop fusion | flops 4325376 | bytes 3670036 | tf_op jit(solution)/shard_map/cond/branch_1_fun/stack | solution.py:55
  153.3 1.1 pad_maximum_fusion.4
  154.4 4.4 %broadcast_in_dim.35 = f32[1,2,2048,512]{3,2,1,0:T(8,128)} broadcast(f32[]{:T(128)} %constant.86.clone.1), dimensions={} | broadcast | bytes 8388612 | tf_op jit(solution)/shard_map/broadcast_in_dim | solution.py:210
  158.7 6.7 %dynamic_update_slice.8 = f32[1,2,2048,512]{3,2,1,0:T(8,128)} dynamic-update-slice(f32[1,2,2048,512]{3,2,1,0:T(8,128)} %broadcast_in_dim.35, f32[1,2,256,256]{3,2,1,0:T(8,128)} %bitcast.74, s32[]{:T(128)} %constant.89.clone.1, s32[]{:T(128)} %constant.89.clone.1, s32[]{:T(128)S(6)} %select_n.117, s32[]{:T(128)S(6)} %select_n.118) | dynamic-update-slice | bytes 1048580 | tf_op jit(solution)/shard_map/dynamic_update_slice | solution.py:214
  165.4 1.5 bitcast_add_fusion.1
  166.9 6.8 %dynamic_update_slice.9 = f32[1,2,2048,512]{3,2,1,0:T(8,128)} dynamic-update-slice(f32[1,2,2048,512]{3,2,1,0:T(8,128)} %dynamic_update_slice.8, f32[1,2,256,256]{3,2,1,0:T(8,128)S(1)} %bitcast_add_fusion.1, s32[]{:T(128)} %constant.89.clone.1, s32[]{:T(128)} %constant.89.clone.1, s32[]{:T(128)S(6)} %select_n.119, s32[]{:T(128)S(6)} %select_n.120) | dynamic-update-slice | bytes 1048580 | tf_op jit(solution)/shard_map/dynamic_update_slice | solution.py:214
  173.7 2.4 %slice.1412 = bf16[1,2,2048,256]{3,2,1,0:T(8,128)(2,1)S(1)} slice(f32[1,2,2048,512]{3,2,1,0:T(8,128)} %dynamic_update_slice.9), slice={[0:1], [0:2], [0:2048], [256:512]} | slice | bytes 4194304 | tf_op jit(solution)/shard_map/slice | solution.py:215
  176.2 46.8 %collective-permute-done.3 = bf16[1,2,2048,256]{3,2,1,0:T(8,128)(2,1)S(1)} collective-permute-done((bf16[1,2,2048,256]{3,2,1,0:T(8,128)(2,1)S(1)}, bf16[1,2,2048,256]{3,2,1,0:T(8,128)(2,1)S(1)}, u32[]{:S(2)}, u32[]{:S(2)}) %collective-permute-start.3) | collective-permute-done | bytes 2097184 | tf_op jit(solution)/shard_map/ppermute | solution.py:12
  223.0 4.1 %fusion.237 = bf16[1,2,2048,256]{3,2,1,0:T(8,128)(2,1)} fusion(f32[1,2,2048,512]{3,2,1,0:T(8,128)} %dynamic_update_slice.9, bf16[1,2,2048,256]{3,2,1,0:T(8,128)(2,1)S(1)} %collective-permute-done.3), kind=kLoop, calls=%fused_computation.360 | loop fusion | flops 3145728 | bytes 8388608 | tf_op jit(solution)/shard_map/convert_element_type | solution.py:218
  (42 shorter events, 11.0 us)
Async XLA Ops:
  0.0 52.1 %collective-permute-start = (bf16[1,2,2048,256]{3,2,1,0:T(8,128)(2,1)}, bf16[1,2,2048,256]{3,2,1,0:T(8,128)(2,1)}, u32[]{:S(2)}, u32[]{:S(2)}) collective-permute-start(bf16[1,2,2048,256]{3,2,1,0:T(8,128)(2,1)} %param.17), channel_id=1, source_target_pairs={{1,0},{2,1},{3,2},{4,3},{5,4},{6,5},{7,6},{8,7},{9,8},{10,9},{11,1... | collective-permute-start | bytes 6291464 | tf_op jit(solution)/shard_map/ppermute | solution.py:12
  56.6 8.2 %copy-start.2 = (f32[5]{0:T(128)S(1)}, f32[5]{0:T(128)}, u32[]{:S(2)}) copy-start(f32[5]{0:T(128)} %param.18) | copy-start | bytes 64
  62.9 0.8 copy-start.1
  81.6 3.1 %collective-permute-start.1 = (bf16[2,2,256,256]{3,2,1,0:T(8,128)(2,1)}, bf16[2,2,256,256]{3,2,1,0:T(8,128)(2,1)}, u32[]{:S(2)}, u32[]{:S(2)}) collective-permute-start(bf16[2,2,256,256]{3,2,1,0:T(8,128)(2,1)} %copy.50), channel_id=1, source_target_pairs={{0,16},{1,17},{2,18},{3,19},{4,20},{5,21},{6,22},{7,23},{8,24},{9,... | collective-permute-start | bytes 1572872 | tf_op jit(solution)/shard_map/while/body/eval_jaxpr/ppermute | solution.py:18
  85.8 1.0 copy-start.5
  87.9 2.1 copy-start.3
  87.9 5.3 %copy-start.4 = (s32[1,2]{1,0:T(1,128)S(1)}, s32[1,2]{1,0:T(1,128)}, u32[]{:S(2)}) copy-start(s32[1,2]{1,0:T(1,128)} %param.22) | copy-start | bytes 28
  88.7 52.6 %collective-permute-start.2 = (bf16[2,2,256,256]{3,2,0,1:T(8,128)(2,1)}, bf16[2,2,256,256]{3,2,0,1:T(8,128)(2,1)S(1)}, u32[]{:S(2)}, u32[]{:S(2)}) collective-permute-start(bf16[2,2,256,256]{3,2,0,1:T(8,128)(2,1)} %get-tuple-element.220), channel_id=1, source_target_pairs={{16,0},{17,1},{18,2},{19,3},{20,4},{21,5},{22,6},{23,7},{24,8},{25... | collective-permute-start | bytes 1572872 | tf_op jit(solution)/shard_map/while/body/eval_jaxpr/ppermute | solution.py:18
  176.1 46.9 %collective-permute-start.3 = (bf16[1,2,2048,256]{3,2,1,0:T(8,128)(2,1)S(1)}, bf16[1,2,2048,256]{3,2,1,0:T(8,128)(2,1)S(1)}, u32[]{:S(2)}, u32[]{:S(2)}) collective-permute-start(bf16[1,2,2048,256]{3,2,1,0:T(8,128)(2,1)S(1)} %slice.1412), channel_id=1, source_target_pairs={{15,0},{0,1},{1,2},{2,3},{3,4},{4,5},{5,6},{6,7},{7,8},{8,9},{9,10... | collective-permute-start | bytes 6291464 | tf_op jit(solution)/shard_map/ppermute | solution.py:12
where the time goes:
time: 229 us; the launch traced here: 227 us
  waiting for transfers between devices  133 us (58%)
  other arithmetic  38.8 us (17%)
  local copies, waits for them, and re-layouts  36.3 us (16%)
  starting transfers between devices  10.4 us (5%)
  between operations  8.33 us (4%)
    ppermute x2, waiting for transfers between devices, from_behind(): return lax.ppermute(block, axis, route)  90.3 us
    ppermute x2, waiting for transfers between devices, passed_along(): return lax.ppermute(shard, axis, pairs)  42.9 us
    dynamic_update_slice x2, local copies, waits for them, and re-layouts, on_device(): accum = lax.dynamic_update_slice(accum, current + grads[slot], corner)  13.5 us
    add x2, other arithmetic, propagate(): imag_part + sign_value * spread_taps(real_part, chirp_taps, axis_pos)  9.48 us
    another operation x2, other arithmetic, propagate(): wavefield = jnp.stack([new_real, new_imag], axis=-3)  7.59 us
    ppermute x2, starting transfers between devices, from_behind(): return lax.ppermute(block, axis, route)  6.99 us
    gather x6, local copies, waits for them, and re-layouts  6.19 us
    another operation x3, other arithmetic, conj_mul(): return jnp.stack([ar * br + ai * bi, ar * bi - ai * br], axis=-3)  5.38 us
  transfers between devices with their start and end apart: 4, of which 4 were waited for; matrix products, arithmetic and copies ran while one was open for 1% of the time, Pallas kernels for 0%

commit v1 on v0

v1 whole, which is shorter than its diff:
```python
import functools
import math

import jax
import jax.numpy as jnp
import numpy as np
from jax import lax
from jax.experimental import pallas as pl
from jax.experimental.pallas import tpu as pltpu
from jax.sharding import PartitionSpec as P

MESH = pl.DeviceIdType.MESH
BF = jnp.bfloat16
F32 = jnp.float32
ALIGN = 16


def dft_tables(length):
    indices = np.arange(length)
    angle = (indices[:, None] * indices[None, :] % length) * (2.0 * math.pi / length)
    factor = 1.0 / math.sqrt(length)
    tables = np.stack([np.cos(angle) * factor, np.sin(angle) * factor])
    return tables.astype(np.float32).astype(jnp.bfloat16)


def dot(first, second):
    return jnp.dot(first, second, preferred_element_type=F32)


def iota(shape, axis):
    return lax.broadcasted_iota(jnp.int32, shape, axis)


def one_hot(shape, offset):
    return jnp.where(iota(shape, 1) == iota(shape, 0) + offset, 1.0, 0.0).astype(BF)


def one_hot_t(shape, offset):
    return jnp.where(iota(shape, 0) == iota(shape, 1) + offset, 1.0, 0.0).astype(BF)


def aligned_start(row, side, height):
    start = jnp.minimum(row // ALIGN * ALIGN, height - side - ALIGN)
    return pl.multiple_of(start, ALIGN)


def propagate(re, im, taps, sign):
    new_re = re - sign * dot(im.astype(BF), taps)
    new_im = im + sign * dot(re.astype(BF), taps)
    out_re = new_re - sign * dot(taps, new_im.astype(BF))
    out_im = new_im + sign * dot(taps, new_re.astype(BF))
    return out_re, out_im


def main_kernel(
    n_tiles,
    rows_ref, cols_ref, counts_ref, taps_ref, rows_any, tr_any, probe_ref, rec_ref, tab_ref,
    left_out, right_out, nrows_out,
    trv, nrows, own_send, own_keep, own_recv, nb_send, nb_recv, lterm, rterm,
    load_sem, pos_send, pos_recv, own_s, own_r, nb_s, nb_r, lt_s, lt_r, rt_s, rt_r, keep_sem,
):
    d = lax.axis_index("depth")
    t = lax.axis_index("tile")
    other = 1 - d
    right = lax.rem(t + 1, n_tiles)
    left = lax.rem(t + n_tiles - 1, n_tiles)
    height = trv.shape[1]
    side = probe_ref.shape[-1]

    load = pltpu.make_async_copy(tr_any, trv, load_sem)
    load.start()

    barrier = pltpu.get_barrier_semaphore()
    for who in ((0, left), (1, left), (0, right), (1, right), (other, t)):
        pl.semaphore_signal(barrier, inc=1, device_id=who, device_id_type=MESH)
    pl.semaphore_wait(barrier, 5)

    pos_copy = pltpu.make_async_remote_copy(
        src_ref=rows_any, dst_ref=nrows, send_sem=pos_send, recv_sem=pos_recv,
        device_id=(d, right), device_id_type=MESH,
    )
    pos_copy.start()

    def rows_at(row, plane):
        block = lax.shift_right_logical(row, side.bit_length() - 1)
        last = height // side - 1
        low = trv[plane, :side, :]
        high = trv[plane, side : 2 * side, :]
        for b in range(1, last + 1):
            after = min(b + 1, last)
            low = jnp.where(block == b, trv[plane, b * side : (b + 1) * side, :], low)
            high = jnp.where(block == b, trv[plane, after * side : (after + 1) * side, :], high)
        shift = row - block * side
        picked = dot(one_hot((side, side), shift), low)
        picked += dot(one_hot((side, side), shift - side), high)
        return picked.astype(BF)

    load.wait()
    row_other = jnp.where(d == 0, rows_ref[0, 1], rows_ref[0, 0])
    row_mine = jnp.where(d == 0, rows_ref[0, 0], rows_ref[0, 1])
    col = jnp.where(d == 0, cols_ref[0, 0], cols_ref[0, 1])
    pos_copy.wait()

    nb_copies = []
    for slot in range(2):
        for plane in range(2):
            nb_send[slot, plane] = rows_at(nrows[0, slot], plane)
        copy = pltpu.make_async_remote_copy(
            src_ref=nb_send.at[slot], dst_ref=nb_recv.at[d],
            send_sem=nb_s.at[slot], recv_sem=nb_r.at[d],
            device_id=(slot, left), device_id_type=MESH,
        )
        copy.start()
        nb_copies.append(copy)
    for plane in range(2):
        own_send[plane] = rows_at(row_other, plane)
    own_copy = pltpu.make_async_remote_copy(
        src_ref=own_send, dst_ref=own_recv, send_sem=own_s, recv_sem=own_r,
        device_id=(other, t), device_id_type=MESH,
    )
    own_copy.start()
    for plane in range(2):
        own_keep[plane] = rows_at(row_mine, plane)
    for slot in range(2):
        nrows_out[0, slot] = nrows[0, slot]

    distance = jnp.abs(iota((side, side), 0) - iota((side, side), 1))
    taps = jnp.zeros((side, side), F32)
    for k in range(taps_ref.shape[0]):
        taps = jnp.where(distance == k, taps_ref[k], taps)
    taps = taps.astype(BF)
    pick_l = one_hot_t((side, side), col)
    pick_r = one_hot_t((side, side), col - side)
    cos, sin = tab_ref[0], tab_ref[1]
    own_copy.wait()

    def window(s):
        pltpu.make_async_remote_copy(
            src_ref=nb_send.at[s], dst_ref=nb_recv.at[s],
            send_sem=nb_s.at[s], recv_sem=nb_r.at[s],
            device_id=(d, left), device_id_type=MESH,
        ).wait_recv()
        mine = jnp.where(d == s, 1.0, 0.0).astype(BF)
        theirs = jnp.where(d == s, 0.0, 1.0).astype(BF)
        parts = []
        for plane in range(2):
            own = own_keep[plane] * mine + own_recv[plane] * theirs
            parts.append(dot(own, pick_l) + dot(nb_recv[s, plane], pick_r))
        return parts

    p_re, p_im = probe_ref[0], probe_ref[1]
    a_re, a_im = window(0)
    u_re, u_im = propagate(a_re * p_re - a_im * p_im, a_re * p_im + a_im * p_re, taps, 1.0)
    u_re, u_im = u_re.astype(BF).astype(F32), u_im.astype(BF).astype(F32)
    b_re, b_im = window(1)
    e_re, e_im = propagate(b_re * u_re - b_im * u_im, b_re * u_im + b_im * u_re, taps, 1.0)
    e_re, e_im = e_re.astype(BF), e_im.astype(BF)
    h_re = (dot(cos, e_re) + dot(sin, e_im)).astype(BF)
    h_im = (dot(cos, e_im) - dot(sin, e_re)).astype(BF)
    f_re = dot(h_re, cos) + dot(h_im, sin)
    f_im = dot(h_im, cos) - dot(h_re, sin)
    live = jnp.where(d < counts_ref[0], 1.0, 0.0)
    misfit = (f_re * f_re + f_im * f_im - rec_ref[d].astype(F32)) * live
    g_re = (misfit * f_re).astype(BF)
    g_im = (misfit * f_im).astype(BF)
    k_re = (dot(cos, g_re) - dot(sin, g_im)).astype(BF)
    k_im = (dot(cos, g_im) + dot(sin, g_re)).astype(BF)
    x_re = dot(k_re, cos) - dot(k_im, sin)
    x_im = dot(k_im, cos) + dot(k_re, sin)

    put_l = one_hot((side, side), col)
    put_r = one_hot((side, side), col - side)
    right_copies = []

    def leave(s, re, im):
        for plane, part in enumerate((re.astype(BF), im.astype(BF))):
            rterm[s, plane] = dot(part, put_r).astype(BF)
        copy = pltpu.make_async_remote_copy(
            src_ref=rterm.at[s], dst_ref=right_out.at[d],
            send_sem=rt_s.at[s], recv_sem=rt_r.at[d],
            device_id=(s, right), device_id_type=MESH,
        )
        copy.start()
        right_copies.append(copy)
        for plane, part in enumerate((re.astype(BF), im.astype(BF))):
            lterm[s, plane] = dot(part, put_l).astype(BF)

    q_re, q_im = propagate(x_re, x_im, taps, -1.0)
    leave(1, u_re * q_re + u_im * q_im, u_re * q_im - u_im * q_re)
    y_re = (b_re * q_re + b_im * q_im).astype(BF).astype(F32)
    y_im = (b_re * q_im - b_im * q_re).astype(BF).astype(F32)
    q_re, q_im = propagate(y_re, y_im, taps, -1.0)
    leave(0, p_re * q_re + p_im * q_im, p_re * q_im - p_im * q_re)

    left_copy = pltpu.make_async_remote_copy(
        src_ref=lterm.at[other], dst_ref=left_out.at[d],
        send_sem=lt_s, recv_sem=lt_r,
        device_id=(other, t), device_id_type=MESH,
    )
    left_copy.start()
    keep = pltpu.make_async_copy(lterm.at[d], left_out.at[d], keep_sem)
    keep.start()
    keep.wait()
    left_copy.wait_send()
    pltpu.make_async_remote_copy(
        src_ref=lterm.at[other], dst_ref=left_out.at[other],
        send_sem=lt_s, recv_sem=lt_r,
        device_id=(other, t), device_id_type=MESH,
    ).wait_recv()
    for copy in nb_copies + right_copies:
        copy.wait_send()
    for slot in range(2):
        pltpu.make_async_remote_copy(
            src_ref=rterm.at[slot], dst_ref=right_out.at[slot],
            send_sem=rt_s.at[slot], recv_sem=rt_r.at[slot],
            device_id=(d, right), device_id_type=MESH,
        ).wait_recv()


def place_kernel(rows_ref, nrows_ref, left_ref, right_ref, out_ref, acc):
    height = out_ref.shape[1]
    side = left_ref.shape[2]
    acc[...] = jnp.zeros_like(acc)
    for blocks, rows in ((left_ref, rows_ref), (right_ref, nrows_ref)):
        for slot in range(2):
            row = rows[0, slot]
            start = aligned_start(row, side, height)
            spread = one_hot_t((side + ALIGN, side), row - start)
            for plane in range(2):
                acc[plane, pl.ds(start, side + ALIGN), :] += dot(spread, blocks[slot, plane])
    out_ref[...] = acc[...].astype(out_ref.dtype)


def on_device(transmission, chirp_taps, probe_field, records, pos_row, pos_col, counts):
    n_tiles = lax.axis_size("tile")
    side = probe_field.shape[-1]
    height, tile_cols = transmission.shape[2:]
    tables = jnp.asarray(dft_tables(side))
    vmem = pl.BlockSpec(memory_space=pltpu.VMEM)
    smem = pl.BlockSpec(memory_space=pltpu.SMEM)
    anywhere = pl.BlockSpec(memory_space=pl.ANY)
    pair = (2, 2, side, side)
    block = (2, side, side)
    dma = pltpu.SemaphoreType.DMA
    left_terms, right_terms, nrows = pl.pallas_call(
        functools.partial(main_kernel, n_tiles),
        out_shape=[
            jax.ShapeDtypeStruct(pair, BF),
            jax.ShapeDtypeStruct(pair, BF),
            jax.ShapeDtypeStruct((1, 2), jnp.int32),
        ],
        in_specs=[smem, smem, smem, smem, anywhere, anywhere, vmem, vmem, vmem],
        out_specs=[anywhere, anywhere, smem],
        scratch_shapes=[
            pltpu.VMEM((2, height, tile_cols), BF),
            pltpu.SMEM((1, 2), jnp.int32),
            pltpu.VMEM(block, BF), pltpu.VMEM(block, BF), pltpu.VMEM(block, BF),
            pltpu.VMEM(pair, BF), pltpu.VMEM(pair, BF),
            pltpu.VMEM(pair, BF), pltpu.VMEM(pair, BF),
            dma, dma, dma, dma, dma, dma((2,)), dma((2,)), dma, dma, dma((2,)), dma((2,)), dma,
        ],
        compiler_params=pltpu.CompilerParams(
            collective_id=0, has_side_effects=True, vmem_limit_bytes=40 * 1024 * 1024
        ),
        name="ptycho_main",
    )(pos_row, pos_col, counts, chirp_taps, pos_row, transmission[0], probe_field, records[0], tables)
    out = pl.pallas_call(
        place_kernel,
        out_shape=jax.ShapeDtypeStruct((2, height, tile_cols), BF),
        in_specs=[smem, smem, vmem, vmem],
        out_specs=vmem,
        scratch_shapes=[pltpu.VMEM((2, height, tile_cols), F32)],
        compiler_params=pltpu.CompilerParams(vmem_limit_bytes=40 * 1024 * 1024),
        name="ptycho_place",
    )(pos_row, nrows, left_terms, right_terms)
    return out[None]


def solution(mesh):
    in_specs = (
        P("depth", None, None, "tile"),
        P(),
        P(),
        P("tile", None, None, None),
        P("tile", None),
        P("tile", None),
        P("tile"),
    )
    out_specs = P("depth", None, None, "tile")
    return jax.shard_map(
        on_device, mesh=mesh, in_specs=in_specs, out_specs=out_specs, check_vma=False
    )
```

time: 229 us -> 49.8 us (0.22)
  waiting for transfers between devices: 133 us -> 0 us
  Pallas kernels: 0 us -> 42.4 us
  other arithmetic: 38.8 us -> 0 us
  local copies, waits for them, and re-layouts: 36.3 us -> 6.49 us
  starting transfers between devices: 10.4 us -> 0 us
  between operations: 8.33 us -> 0.67 us
    ppermute x4 -> x0, waiting for transfers between devices: 133 us -> none  [the longest x2 90.3 us: from_behind(): return lax.ppermute(block, axis, route)]
    pallas_call x0 -> x2, Pallas kernels: none -> 42.4 us  [the longest x1 39.6 us: on_device(): pl.pallas_call(functools.partial(main_kernel, n_tiles), out_shape=[jax.Sh...]
    dynamic_update_slice x2 -> x0, local copies, waits for them, and re-layouts: 13.5 us -> none  [on_device(): accum = lax.dynamic_update_slice(accum, current + grads[slot], corner)]
    another operation x5 -> x0, other arithmetic: 13 us -> none  [the longest x2 7.59 us: propagate(): wavefield = jnp.stack([new_real, new_imag], axis=-3)]
    add x3 -> x0, other arithmetic: 11 us -> none  [the longest x2 9.48 us: propagate(): imag_part + sign_value * spread_taps(real_part, chirp_taps, axis_pos)]
    ppermute x4 -> x0, starting transfers between devices: 10.4 us -> none  [the longest x2 6.99 us: from_behind(): return lax.ppermute(block, axis, route)]
    convert_element_type x6 -> x0, other arithmetic: 7.62 us -> none  [the longest x1 4.13 us: on_device(): return (accum[..., :tile_cols] + from_left).astype(jnp.bfloat16)]
    broadcast_in_dim x5 -> x0, local copies, waits for them, and re-layouts: 6.37 us -> none  [the longest x1 4.36 us: on_device(): jnp.zeros((slices_here, 2, transmission.shape[2], 2 * tile_cols), jnp.flo...]
  transfers between devices with their start and end apart: 4 -> 0, of which waited for: 4 -> 0; matrix products, arithmetic and copies ran while one was open for 1% -> 0% of each run, Pallas kernels for 0% -> 0%
where the time goes in v1:
time: 49.8 us; the launch traced here: 49.5 us
  Pallas kernels  42.4 us (85%)
  local copies, waits for them, and re-layouts  6.49 us (13%)
  between operations  0.67 us (1%)
    pallas_call x1, Pallas kernels, on_device(): pl.pallas_call(functools.partial(main_kernel, n_tiles), out_shape=[jax.Sh...  39.6 us
    unnamed x14, local copies, waits for them, and re-layouts  6.49 us
    pallas_call x1, Pallas kernels, on_device(): pl.pallas_call(place_kernel, out_shape=jax.ShapeDtypeStruct((2, height, t...  2.8 us

profile of v1, /device:TPU:0, one launch (start us, length us, event | category | flops | bytes accessed | tf_op | source)
XLA Modules:
  0.0 49.5 jit_solution(15317089124482031770)
XLA Ops:
  0.7 0.0 copy-start
  0.7 1.6 %copy-done = bf16[1,2,2048,256]{3,2,1,0:T(8,128)(2,1)S(1)} copy-done((bf16[1,2,2048,256]{3,2,1,0:T(8,128)(2,1)S(1)}, bf16[1,2,2048,256]{3,2,1,0:T(8,128)(2,1)}, u32[]{:S(2)}) %copy-start) | copy-done | bytes 2097176
  2.2 0.0 copy-start.1
  2.2 1.0 %copy-done.1 = f32[2,256,256]{2,1,0:T(8,128)S(1)} copy-done((f32[2,256,256]{2,1,0:T(8,128)S(1)}, f32[2,256,256]{2,1,0:T(8,128)}, u32[]{:S(2)}) %copy-start.1) | copy-done | bytes 524312
  3.3 0.0 copy-start.2
  3.3 0.9 %copy-done.2 = bf16[1,2,256,256]{3,2,1,0:T(8,128)(2,1)S(1)} copy-done((bf16[1,2,256,256]{3,2,1,0:T(8,128)(2,1)S(1)}, bf16[1,2,256,256]{3,2,1,0:T(8,128)(2,1)}, u32[]{:S(2)}) %copy-start.2) | copy-done | bytes 262168
  4.2 0.0 copy-start.3
  4.2 0.9 %copy-done.3 = bf16[2,256,256]{2,1,0:T(8,128)(2,1)S(1)} copy-done((bf16[2,256,256]{2,1,0:T(8,128)(2,1)S(1)}, bf16[2,256,256]{2,1,0:T(8,128)(2,1)}, u32[]{:S(2)}) %copy-start.3) | copy-done | bytes 262168
  5.2 0.0 copy-start.4
  5.2 0.7 %copy-done.4 = s32[1,2]{1,0:T(1,128)S(1)} copy-done((s32[1,2]{1,0:T(1,128)S(1)}, s32[1,2]{1,0:T(1,128)}, u32[]{:S(2)}) %copy-start.4) | copy-done | bytes 32
  5.8 0.0 copy-start.5
  5.8 0.7 %copy-done.5 = s32[1,2]{1,0:T(1,128)S(1)} copy-done((s32[1,2]{1,0:T(1,128)S(1)}, s32[1,2]{1,0:T(1,128)}, u32[]{:S(2)}) %copy-start.5) | copy-done | bytes 32
  6.5 0.0 copy-start.6
  6.5 0.7 %copy-done.6 = f32[5]{0:T(128)S(1)} copy-done((f32[5]{0:T(128)S(1)}, f32[5]{0:T(128)}, u32[]{:S(2)}) %copy-start.6) | copy-done | bytes 44
  7.2 39.6 %ptycho_main.1 = (bf16[2,2,256,256]{3,2,1,0:T(8,128)(2,1)S(1)}, bf16[2,2,256,256]{3,2,1,0:T(8,128)(2,1)S(1)}, s32[1,2]{1,0:T(1,128)S(1)}) custom-call(s32[1,2]{1,0:T(1,128)S(1)} %copy-done.4, s32[1,2]{1,0:T(1,128)S(1)} %copy-done.5, s32[1]{0:T(128)S(6)} %copy.9.counts_ref, f32[5]{0:T(128)S(1)} %copy-done.6, s32[1,2]{1,0:T(1,128)S(1)} %copy-done.4, ...), custom_call_target="tpu_custom_call" | custom-call | tf_op jit(solution)/shard_map/ptycho_main/pallas_call | solution.py:245
  46.7 2.8 %ptycho_place.1 = bf16[2,2048,256]{2,1,0:T(8,128)(2,1)} custom-call(s32[1,2]{1,0:T(1,128)S(1)} %copy-done.4, s32[1,2]{1,0:T(1,128)S(1)} %get-tuple-element.8.nrows_ref, bf16[2,2,256,256]{3,2,1,0:T(8,128)(2,1)S(1)} %get-tuple-element.9.left_ref, bf16[2,2,256,256]{3,2,1,0:T(8,128)(2,1)S(1)} %get-tuple-element.10.right_ref), custom_call_target="tpu_custom_call" | custom-call | tf_op jit(solution)/shard_map/ptycho_place/pallas_call | solution.py:267
Async XLA Ops:
  0.7 1.6 %copy-start = (bf16[1,2,2048,256]{3,2,1,0:T(8,128)(2,1)S(1)}, bf16[1,2,2048,256]{3,2,1,0:T(8,128)(2,1)}, u32[]{:S(2)}) copy-start(bf16[1,2,2048,256]{3,2,1,0:T(8,128)(2,1)} %param.8) | copy-start | bytes 6291460
  2.2 1.0 %copy-start.1 = (f32[2,256,256]{2,1,0:T(8,128)S(1)}, f32[2,256,256]{2,1,0:T(8,128)}, u32[]{:S(2)}) copy-start(f32[2,256,256]{2,1,0:T(8,128)} %probe_ref.1) | copy-start | bytes 1572868
  3.3 0.9 %copy-start.2 = (bf16[1,2,256,256]{3,2,1,0:T(8,128)(2,1)S(1)}, bf16[1,2,256,256]{3,2,1,0:T(8,128)(2,1)}, u32[]{:S(2)}) copy-start(bf16[1,2,256,256]{3,2,1,0:T(8,128)(2,1)} %param.11) | copy-start | bytes 786436
  4.2 0.9 %copy-start.3 = (bf16[2,256,256]{2,1,0:T(8,128)(2,1)S(1)}, bf16[2,256,256]{2,1,0:T(8,128)(2,1)}, u32[]{:S(2)}) copy-start(bf16[2,256,256]{2,1,0:T(8,128)(2,1)} %constant.2.clone.tab_ref) | copy-start | bytes 786436
  5.2 0.7 %copy-start.4 = (s32[1,2]{1,0:T(1,128)S(1)}, s32[1,2]{1,0:T(1,128)}, u32[]{:S(2)}) copy-start(s32[1,2]{1,0:T(1,128)} %rows_ref.3) | copy-start | bytes 28
  5.8 0.7 %copy-start.5 = (s32[1,2]{1,0:T(1,128)S(1)}, s32[1,2]{1,0:T(1,128)}, u32[]{:S(2)}) copy-start(s32[1,2]{1,0:T(1,128)} %cols_ref.1) | copy-start | bytes 28
  6.5 0.7 %copy-start.6 = (f32[5]{0:T(128)S(1)}, f32[5]{0:T(128)}, u32[]{:S(2)}) copy-start(f32[5]{0:T(128)} %taps_ref.1) | copy-start | bytes 64
